TPU v7x, 32 devices: a whole 2x2x4 slice. The times are simulated.
32 devices in a mesh: seg: 4 (over x, core), tr: 8 (over z, y).
Axes of the slice: x: 2, y: 2, z: 4, core: 2. Of those that a mesh axis runs over, the one named last changes fastest.
Arguments:
- energies: float32 [1], replicated, may hold values from -0.1 to 0.1
- hamiltonian: bfloat16 [8, 768, 768], P('seg'), may hold values from -4 to 4
- coupling: bfloat16 [8, 768, 768], P('seg'), may hold values from -1.5 to 1.5
- seed_inverse: bfloat16 [2, 1, 8, 768, 768], P(None, None, 'seg'), may hold values from -2 to 2
- lead_green: bfloat16 [2, 1, 768, 768], P(None, None, None, 'tr'), may hold values from -1 to 1
Outputs:
- green: bfloat16 [2, 1, 8, 768, 768], P(None, None, 'seg', None, 'tr')
All inputs are finite; a program needn't handle non-finite values.
Results may differ from a plain program's by a relative error of at most 0.025.
Values may be sent and summed in bfloat16 or wider, within the bound.
A program may use at most 64 MiB of HBM per device.

v0:
```python
import jax
import jax.numpy as jnp
from jax import lax
from jax.sharding import PartitionSpec as P

broadening = 0.6


def passed_along(value, axis, steps):
    count = lax.axis_size(axis)
    leading, last = (max(0, -steps), min(count, count - steps))
    return lax.ppermute(value, axis, [(source, source + steps) for source in range(leading, last)])


def product(left, right):
    return jnp.dot(left, right, preferred_element_type=jnp.float32)


def pair_product(left_real, left_imag, right_real, right_imag):
    real_part = product(left_real, right_real) - product(left_imag, right_imag)
    imag_part = product(left_real, right_imag) + product(left_imag, right_real)
    return (real_part, imag_part)


def local(energies, hamiltonian, coupling, seed_inverse, lead_green):
    seg_count = lax.axis_size("seg")
    seg_place = lax.axis_index("seg")
    width = lead_green.shape[3]
    order = lead_green.shape[2]
    col_start = lax.axis_index("tr") * width
    energy_count = energies.shape[0]
    slab_count = hamiltonian.shape[0]

    def columns(block):
        return lax.dynamic_slice_in_dim(block, col_start, width, 1)

    def weights_of(seeds, slab_index):
        couple = coupling[slab_index]
        local_real = columns(seeds[0, slab_index])
        local_imag = columns(seeds[1, slab_index])
        weight_real = jnp.einsum(
            "kb,kc->bc", couple, local_real, preferred_element_type=jnp.float32
        )
        weight_imag = jnp.einsum(
            "kb,kc->bc", couple, local_imag, preferred_element_type=jnp.float32
        )
        return jnp.stack([weight_real, weight_imag]).astype(jnp.bfloat16)

    def bias_of(energy, seeds, slab_index):
        onsite = hamiltonian[slab_index]
        local_real = columns(seeds[0, slab_index])
        local_imag = columns(seeds[1, slab_index])
        real32 = local_real.astype(jnp.float32)
        imag32 = local_imag.astype(jnp.float32)
        bias_real = energy * real32 - broadening * imag32 - product(onsite, local_real)
        bias_imag = energy * imag32 + broadening * real32 - product(onsite, local_imag)
        return jnp.stack([bias_real, bias_imag])

    def fold_columns(shard, weights):
        piece = lax.all_gather(shard, "tr", axis=2, tiled=True)
        part_real, part_imag = pair_product(piece[0], piece[1], weights[0], weights[1])
        return jnp.stack([part_real, part_imag]).astype(jnp.bfloat16)

    def finish(seeds, slab_index, carried, bias):
        couple = coupling[slab_index]
        probe_real = (bias[0] - product(couple, carried[0])).astype(jnp.bfloat16)
        probe_imag = (bias[1] - product(couple, carried[1])).astype(jnp.bfloat16)
        back_real, back_imag = pair_product(
            seeds[0, slab_index], seeds[1, slab_index], probe_real, probe_imag
        )
        local_real = columns(seeds[0, slab_index]).astype(jnp.float32)
        local_imag = columns(seeds[1, slab_index]).astype(jnp.float32)
        green_real = (2.0 * local_real - back_real).astype(jnp.bfloat16)
        green_imag = (2.0 * local_imag - back_imag).astype(jnp.bfloat16)
        return jnp.stack([green_real, green_imag])

    weight_table = jnp.stack(
        [
            jnp.stack(
                [weights_of(seed_inverse[:, 0], slab_index) for slab_index in range(slab_count)]
            )
        ]
    )
    bias_table = jnp.stack(
        [
            jnp.stack(
                [
                    bias_of(energies[0], seed_inverse[:, 0], slab_index)
                    for slab_index in range(slab_count)
                ]
            )
        ]
    )

    def weights_at(energy_index, slab_index):
        chosen = lax.dynamic_index_in_dim(weight_table, energy_index, 0, False)[slab_index]
        return chosen

    def bias_at(energy_index, slab_index):
        chosen = lax.dynamic_index_in_dim(bias_table, energy_index, 0, False)[slab_index]
        return chosen

    def settle(working, onward, stored, blocks, energy_index):
        recorded = lax.dynamic_update_index_in_dim(stored, blocks, energy_index, 1)
        kept = jnp.where(working, recorded, stored)
        sent = jnp.where(working, onward, jnp.zeros_like(onward))
        return (sent, kept)

    def section_setup(section):
        energy_raw = section - seg_place
        energy_index = jnp.clip(energy_raw, 0, energy_count - 1)
        energy = lax.dynamic_index_in_dim(energies, energy_index, 0, False)
        seeds = lax.dynamic_index_in_dim(seed_inverse, energy_index, 1, False)
        working = jnp.logical_and(energy_raw >= 0, energy_raw < energy_count)
        return (working, energy_index, energy, seeds)

    green_init = jnp.zeros((2, energy_count, slab_count, order, width), jnp.bfloat16)
    last_init = jnp.zeros((2, order, width), jnp.bfloat16)
    section_total = seg_count + energy_count - 1

    def section_step(section, state):
        last_block, green_out = state
        working, energy_index, energy, seeds = section_setup(section)
        incoming = passed_along(last_block, "seg", 1)
        lead_block = lax.dynamic_index_in_dim(lead_green, energy_index, 1, False)
        current = jnp.where(seg_place == 0, lead_block, incoming)
        blocks = []
        for slab_index in range(slab_count):
            carried = fold_columns(current, weights_at(energy_index, slab_index))
            current = finish(seeds, slab_index, carried, bias_at(energy_index, slab_index))
            blocks.append(current)
        return settle(working, current, green_out, jnp.stack(blocks, axis=1), energy_index)

    final = lax.fori_loop(0, section_total, section_step, (last_init, green_init))
    return final[1]


def solution(mesh):
    in_specs = (
        P(),
        P("seg", None, None),
        P("seg", None, None),
        P(None, None, "seg", None, None),
        P(None, None, None, "tr"),
    )
    out_specs = P(None, None, "seg", None, "tr")
    return jax.shard_map(local, mesh=mesh, in_specs=in_specs, out_specs=out_specs, check_vma=False)
```

profile of v0, /device:TPU:3, one launch (start us, length us, event | category | flops | bytes accessed | tf_op | source)
XLA Modules:
  0.0 623.6 jit_solution(3056923825078450821)
XLA Ops:
  6.5 6.6 %copy.6 = bf16[2,1,2,768,768]{3,4,2,0,1:T(8,128)(2,1)} copy(bf16[2,1,2,768,768]{4,3,2,1,0:T(8,128)(2,1)} %param.10) | data formatting | bytes 9437184 | tf_op args[3]
  13.2 2.8 fusion.199
  21.3 1.9 fusion.146
  25.4 590.5 %while.18 = (s32[]{:T(128)}, bf16[2,768,96]{1,2,0:T(8,128)(2,1)S(1)}, bf16[2,1,2,768,96]{3,4,0,2,1:T(8,128)(2,1)S(1)}, s32[]{:T(128)}, bf16[1,1,768,96]{2,3,1,0:...) while((s32[]{:T(128)}, ...), condition=%wide.region_1.2_spmd.clone, body=%wide.region_0.1_spmd.clone.sunk | while | flops 2269200384 | bytes 56426808 | solution.py:134
  26.7 2.4 collective-permute-done
  29.9 56.6 %all-gather.3.cloned.1.call-done = bf16[2,768,768]{1,2,0:T(8,128)(2,1)} async-done(((bf16[2,768,96]{1,2,0:T(8,128)(2,1)}), bf16[2,768,768]{1,2,0:T(8,128)(2,1)}) %all-gather.3.cloned.1.call-update) | async-done | bytes 2359312 | tf_op jit(solution)/shard_map/while/body/eval_jaxpr/all_gather | solution.py:60
  86.5 1.8 fusion.270
  88.3 3.1 fusion.271
  93.2 2.5 fusion.267
  95.7 2.8 fusion.268
  100.4 1.8 fusion.274
  102.1 1.8 fusion.272
  104.7 50.8 %all-gather.5.cloned.1.call-done = bf16[2,768,768]{1,2,0:T(8,128)(2,1)} async-done(((bf16[2,768,96]{1,2,0:T(8,128)(2,1)}), bf16[2,768,768]{1,2,0:T(8,128)(2,1)}) %all-gather.5.cloned.1.call-update) | async-done | bytes 2359312 | tf_op jit(solution)/shard_map/while/body/eval_jaxpr/all_gather | solution.py:60
  155.5 2.5 fusion.279
  158.0 3.2 fusion.280
  163.0 2.5 fusion.276
  165.6 2.8 fusion.277
  170.2 1.8 fusion.283
  172.0 1.8 fusion.281
  175.5 3.6 collective-permute-done
  179.9 53.9 %all-gather.3.cloned.1.call-done = bf16[2,768,768]{1,2,0:T(8,128)(2,1)} async-done(((bf16[2,768,96]{1,2,0:T(8,128)(2,1)}), bf16[2,768,768]{1,2,0:T(8,128)(2,1)}) %all-gather.3.cloned.1.call-update) | async-done | bytes 2359312 | tf_op jit(solution)/shard_map/while/body/eval_jaxpr/all_gather | solution.py:60
  233.8 1.8 fusion.270
  235.6 3.1 fusion.271
  240.5 2.5 fusion.267
  243.0 2.8 fusion.268
  247.6 1.8 fusion.274
  249.4 1.8 fusion.272
  252.0 50.8 %all-gather.5.cloned.1.call-done = bf16[2,768,768]{1,2,0:T(8,128)(2,1)} async-done(((bf16[2,768,96]{1,2,0:T(8,128)(2,1)}), bf16[2,768,768]{1,2,0:T(8,128)(2,1)}) %all-gather.5.cloned.1.call-update) | async-done | bytes 2359312 | tf_op jit(solution)/shard_map/while/body/eval_jaxpr/all_gather | solution.py:60
  302.8 2.5 fusion.279
  305.3 3.2 fusion.280
  310.3 2.5 fusion.276
  312.9 2.8 fusion.277
  317.5 1.8 fusion.283
  319.3 1.8 fusion.281
  322.8 3.5 collective-permute-done
  327.1 53.9 %all-gather.3.cloned.1.call-done = bf16[2,768,768]{1,2,0:T(8,128)(2,1)} async-done(((bf16[2,768,96]{1,2,0:T(8,128)(2,1)}), bf16[2,768,768]{1,2,0:T(8,128)(2,1)}) %all-gather.3.cloned.1.call-update) | async-done | bytes 2359312 | tf_op jit(solution)/shard_map/while/body/eval_jaxpr/all_gather | solution.py:60
  381.0 1.8 fusion.270
  382.8 3.1 fusion.271
  387.7 2.5 fusion.267
  390.3 2.8 fusion.268
  394.9 1.8 fusion.274
  396.7 1.8 fusion.272
  399.3 50.8 %all-gather.5.cloned.1.call-done = bf16[2,768,768]{1,2,0:T(8,128)(2,1)} async-done(((bf16[2,768,96]{1,2,0:T(8,128)(2,1)}), bf16[2,768,768]{1,2,0:T(8,128)(2,1)}) %all-gather.5.cloned.1.call-update) | async-done | bytes 2359312 | tf_op jit(solution)/shard_map/while/body/eval_jaxpr/all_gather | solution.py:60
  450.0 2.5 fusion.279
  452.6 3.2 fusion.280
  457.6 2.5 fusion.276
  460.1 2.8 fusion.277
  464.8 1.8 fusion.283
  466.5 1.8 fusion.281
  470.0 3.5 collective-permute-done
  474.4 53.9 %all-gather.3.cloned.1.call-done = bf16[2,768,768]{1,2,0:T(8,128)(2,1)} async-done(((bf16[2,768,96]{1,2,0:T(8,128)(2,1)}), bf16[2,768,768]{1,2,0:T(8,128)(2,1)}) %all-gather.3.cloned.1.call-update) | async-done | bytes 2359312 | tf_op jit(solution)/shard_map/while/body/eval_jaxpr/all_gather | solution.py:60
  528.3 1.8 fusion.270
  530.1 3.1 fusion.271
  535.0 2.5 fusion.267
  537.6 2.8 fusion.268
  542.2 1.8 fusion.274
  544.0 1.8 fusion.272
  546.5 50.8 %all-gather.5.cloned.1.call-done = bf16[2,768,768]{1,2,0:T(8,128)(2,1)} async-done(((bf16[2,768,96]{1,2,0:T(8,128)(2,1)}), bf16[2,768,768]{1,2,0:T(8,128)(2,1)}) %all-gather.5.cloned.1.call-update) | async-done | bytes 2359312 | tf_op jit(solution)/shard_map/while/body/eval_jaxpr/all_gather | solution.py:60
  597.3 2.5 fusion.279
  599.8 3.2 fusion.280
  604.9 2.5 fusion.276
  607.4 2.8 fusion.277
  612.0 1.8 fusion.283
  613.8 1.8 fusion.281
  (79 shorter events, 48.8 us)
Async XLA Ops:
  13.2 3.1 copy-start.2
  21.3 2.0 copy-start.1
  24.4 1.0 copy-start
  25.4 61.1 %all-gather.3.cloned.1.call-start = ((), (), s32[]{:S(2)}) async-start(), calls=%async_computation | async-start | bytes 2654208 | tf_op jit(solution)/shard_map/while/body/eval_jaxpr/all_gather | solution.py:60
  25.4 3.7 collective-permute-start
  29.8 125.6 %all-gather.5.cloned.1.call-start = ((), (), s32[]{:S(2)}) async-start(), calls=%async_computation.1 | async-start | bytes 2654208 | tf_op jit(solution)/shard_map/while/body/eval_jaxpr/all_gather | solution.py:60
  174.1 59.7 %all-gather.3.cloned.1.call-start = ((), (), s32[]{:S(2)}) async-start(), calls=%async_computation | async-start | bytes 2654208 | tf_op jit(solution)/shard_map/while/body/eval_jaxpr/all_gather | solution.py:60
  174.2 4.9 collective-permute-start
  179.8 122.9 %all-gather.5.cloned.1.call-start = ((), (), s32[]{:S(2)}) async-start(), calls=%async_computation.1 | async-start | bytes 2654208 | tf_op jit(solution)/shard_map/while/body/eval_jaxpr/all_gather | solution.py:60
  321.4 59.7 %all-gather.3.cloned.1.call-start = ((), (), s32[]{:S(2)}) async-start(), calls=%async_computation | async-start | bytes 2654208 | tf_op jit(solution)/shard_map/while/body/eval_jaxpr/all_gather | solution.py:60
  321.5 4.8 collective-permute-start
  327.1 122.9 %all-gather.5.cloned.1.call-start = ((), (), s32[]{:S(2)}) async-start(), calls=%async_computation.1 | async-start | bytes 2654208 | tf_op jit(solution)/shard_map/while/body/eval_jaxpr/all_gather | solution.py:60
  468.7 59.7 %all-gather.3.cloned.1.call-start = ((), (), s32[]{:S(2)}) async-start(), calls=%async_computation | async-start | bytes 2654208 | tf_op jit(solution)/shard_map/while/body/eval_jaxpr/all_gather | solution.py:60
  468.7 4.8 collective-permute-start
  474.4 122.9 %all-gather.5.cloned.1.call-start = ((), (), s32[]{:S(2)}) async-start(), calls=%async_computation.1 | async-start | bytes 2654208 | tf_op jit(solution)/shard_map/while/body/eval_jaxpr/all_gather | solution.py:60
Sparse Core Ops, SparseCore 0:
  29.9 56.4 all-gather.2
  104.8 50.6 all-gather.4
  179.9 53.7 all-gather.2
  252.1 50.6 all-gather.4
  327.2 53.7 all-gather.2
  399.4 50.6 all-gather.4
  474.5 53.7 all-gather.2
  546.7 50.6 all-gather.4
where the time goes:
time: 629 us; the launch traced here: 624 us
  waiting for transfers between devices  435 us (69%)
  matrix products  149 us (24%)
  between operations  14.2 us (2%)
  local copies, waits for them, and re-layouts  12.6 us (2%)
  other arithmetic  7.53 us (1%)
    all_gather x8, waiting for transfers between devices, fold_columns(): piece = lax.all_gather(shard, 'tr', axis=2, tiled=True)  421 us
    dot_general x68, matrix products, product(): return jnp.dot(left, right, preferred_element_type=jnp.float32)  147 us
    ppermute x4, waiting for transfers between devices, passed_along(): lax.ppermute(value, axis, [(source, source + steps) for source in range(l...  13 us
  transfers between devices with their start and end apart: 12, of which 12 were waited for; matrix products, arithmetic and copies ran while one was open for 0% of the time, Pallas kernels for 0%

commit v1 on v0

v1 whole, which is shorter than its diff:
```python
import functools

import jax
import jax.numpy as jnp
from jax import lax
from jax.experimental import pallas as pl
from jax.experimental.pallas import tpu as pltpu
from jax.sharding import PartitionSpec as P

broadening = 0.6
LANES = 128


def mm(left, right):
    return jnp.dot(left, right, preferred_element_type=jnp.float32)


def pick(index, values):
    total = jnp.int32(0)
    for place, value in enumerate(values):
        total = total + jnp.where(index == place, jnp.int32(value), jnp.int32(0))
    return total


def kernel(
    nseg, n, width, pad,
    energies, ham, cpl, seed, lead, out,
    ct, gath, mix, vec, uvec, bias, acc, car,
    vs_sem, vr_sem, cs_sem, cr_sem, gs_sem, gr_sem, fs_sem, fr_sem, bs_sem, br_sem,
):
    slabs = ham.shape[0]
    order = ham.shape[1]
    half = order // 2
    steps = n // 2
    ticks = 2 * steps
    wide = 2 * pad
    chains = 2 * slabs
    seg = lax.axis_index("seg")
    tr = lax.axis_index("tr")
    role = seg % 2
    low = role == 0
    high = role == 1
    first = seg == 0
    partner = seg + 1 - 2 * role
    linked = jnp.logical_and(high, seg + 1 < nseg)
    fed = jnp.logical_and(low, seg > 0)

    def place_of(t):
        odd = t % 2
        return odd * (n - 1 - t // 2) + (1 - odd) * (t // 2)

    def tr_at(position):
        position = (position + 2 * n) % n
        past = position // steps
        return (1 - past) * (2 * position) + past * (2 * (n - 1 - position) + 1)

    me = place_of(tr)
    following, preceding = tr_at(me + 1), tr_at(me - 1)

    barrier = pltpu.get_barrier_semaphore()

    def greet(s, t):
        pl.semaphore_signal(
            barrier, inc=1, device_id=(s, t), device_id_type=pl.DeviceIdType.MESH
        )

    greet(partner, tr)

    @pl.when(low)
    def _():
        greet(seg, following)
        greet(seg, preceding)

    @pl.when(fed)
    def _():
        greet(seg - 1, tr)

    @pl.when(linked)
    def _():
        greet(seg + 1, tr)

    peers = 1 + 2 * (1 - role) + jnp.where(jnp.logical_or(fed, linked), 1, 0)
    pl.semaphore_wait(barrier, peers)

    def remote(src, dst, send, recv, s, t):
        return pltpu.make_async_remote_copy(
            src_ref=src, dst_ref=dst, send_sem=send, recv_sem=recv,
            device_id=(s, t), device_id_type=pl.DeviceIdType.MESH,
        )

    def ring_next(s, h):
        owner = tr_at(me - s)
        return remote(
            gath.at[owner, h], gath.at[owner, h], fs_sem.at[s, h], fr_sem.at[s, h], seg, following
        )

    def ring_prev(s, h):
        owner = tr_at(me + s)
        return remote(
            gath.at[owner, h], gath.at[owner, h], bs_sem.at[s, h], br_sem.at[s, h], seg, preceding
        )

    def goes_next(s, h):
        return jnp.logical_or(s < steps - 1, h == 0)

    def goes_prev(s, h):
        return jnp.logical_or(s < steps - 1, h == 1)

    def ring_start(s, h):
        @pl.when(goes_next(s, h))
        def _():
            ring_next(s, h).start()

        @pl.when(goes_prev(s, h))
        def _():
            ring_prev(s, h).start()

    def tick(j):
        s, h = j // 2, j % 2

        @pl.when(goes_next(s, h))
        def _():
            ring_next(s, h).wait_recv()

        @pl.when(goes_prev(s, h))
        def _():
            ring_prev(s, h).wait_recv()

        @pl.when(s + 1 < steps)
        def _():
            ring_start(s + 1, h)

    def send_vec(k):
        return remote(
            vec.at[k], vec.at[slabs + k], vs_sem.at[k], vr_sem.at[k], partner, tr
        )

    def send_car(k):
        return remote(
            car.at[slabs + k], car.at[k], cs_sem.at[k], cr_sem.at[k], partner, tr
        )

    def send_block(h, s):
        return remote(
            car.at[slabs - 1, pl.ds(h * half, half)], gath.at[tr, h],
            gs_sem.at[h], gr_sem.at[h], s, tr,
        )

    @pl.when(first)
    def _():
        for h in range(2):
            rows = slice(h * half, (h + 1) * half)
            gath[tr, h] = jnp.zeros((half, wide), jnp.bfloat16)
            gath[tr, h, :, 0:width] = lead[0, 0, rows, :]
            gath[tr, h, :, pad : pad + width] = lead[1, 0, rows, :]
            ring_start(0, h)

    row = lax.broadcasted_iota(jnp.int32, (order, wide), 0)
    lane = lax.broadcasted_iota(jnp.int32, (order, wide), 1)
    chosen = jnp.logical_and(row == tr * width + lane, lane < width)
    unit = jnp.where(chosen, 1.0, 0.0).astype(jnp.bfloat16)
    for k in range(slabs):
        vec[k] = unit
        ct[k] = jnp.transpose(cpl[k])

    energy = energies[0]

    def times_seed(b, value):
        by_real = mm(seed[0, 0, b], value)
        by_imag = mm(seed[1, 0, b], value)
        real = by_real[:, :pad] - by_imag[:, pad:]
        imag = by_real[:, pad:] + by_imag[:, :pad]
        return jnp.concatenate([real, imag], axis=1)

    own_back = [(k, b) for k in reversed(range(slabs)) for b in reversed(range(k + 1))]
    far = [(slabs + k, b) for k in reversed(range(slabs)) for b in reversed(range(slabs))]
    back = own_back + far
    own_count, far_count = len(own_back), len(far)

    def back_pass(i, carry):
        k = pick(i, [item[0] for item in back])
        b = pick(i, [item[1] for item in back])
        for index, (chain, slab) in enumerate(far):
            if slab == slabs - 1:
                @pl.when(i == own_count + index)
                def _(chain=chain):
                    send_vec(chain - slabs).wait_recv()

        u = times_seed(b, vec[k]).astype(jnp.bfloat16)
        uvec[k, b] = u
        onsite = mm(ham[b], u)
        vec[k] = mm(ct[b], u).astype(jnp.bfloat16)
        u32 = u.astype(jnp.float32)
        real, imag = u32[:, :pad], u32[:, pad:]
        turned = jnp.concatenate([-imag, real], axis=1)
        bias[k, b] = energy * u32 + broadening * turned - onsite
        for index, (chain, slab) in enumerate(own_back):
            if slab == 0:
                @pl.when(jnp.logical_and(high, i == index))
                def _(chain=chain):
                    send_vec(chain).start()

        @pl.when(jnp.logical_and(first, i < ticks))
        def _():
            tick(i)

        return carry

    lax.fori_loop(0, own_count + (1 - role) * far_count, back_pass, 0)

    @pl.when(first)
    def _():
        def rest(j, carry):
            tick(j)
            return carry

        lax.fori_loop(min(own_count + far_count, ticks), ticks, rest, 0)

    @pl.when(low)
    def _():
        def build(t, carry):
            mix[t] = jnp.zeros((wide, chains * wide), jnp.bfloat16)
            rows = pl.ds(pl.multiple_of(t * width, 16), width)
            for k in range(chains):
                block = vec[k, rows, :]
                real, imag = block[:, :pad], block[:, pad:]
                base = k * wide
                mix[t, 0:width, base : base + wide] = block
                mix[t, pad : pad + width, base : base + pad] = -imag
                mix[t, pad : pad + width, base + pad : base + wide] = real
            return carry

        lax.fori_loop(0, n, build, 0)

        for h in range(2):
            @pl.when(fed)
            def _(h=h):
                send_block(h, seg).wait_recv()
                ring_start(0, h)

        for h in range(2):
            acc[h] = mm(gath[tr, h], mix[tr])

        def add(owner, h):
            acc[h] = acc[h] + mm(gath[owner, h], mix[owner])

        def arrive(j, carry):
            @pl.when(fed)
            def _():
                tick(j)

            s, h = j // 2, j % 2

            @pl.when(goes_next(s, h))
            def _():
                add(tr_at(me - 1 - s), h)

            @pl.when(goes_prev(s, h))
            def _():
                add(tr_at(me + 1 + s), h)

            return carry

        lax.fori_loop(0, ticks, arrive, 0)
        for k in range(chains):
            for h in range(2):
                car[k, h * half : (h + 1) * half, :] = acc[
                    h, :, k * wide : (k + 1) * wide
                ].astype(jnp.bfloat16)

    far_on = [(slabs + k, b) for k in reversed(range(slabs)) for b in range(slabs)]
    own_on = [(k, b) for k in reversed(range(slabs)) for b in range(k + 1)]
    onward = far_on + own_on

    def on_pass(i, carry):
        k = pick(i, [item[0] for item in onward])
        b = pick(i, [item[1] for item in onward])
        for index, (chain, slab) in enumerate(own_on):
            if slab == 0:
                @pl.when(jnp.logical_and(high, i == far_count + index))
                def _(chain=chain):
                    send_car(chain).wait_recv()

        probe = (bias[k, b] - mm(cpl[b], car[k])).astype(jnp.bfloat16)
        green = 2.0 * uvec[k, b].astype(jnp.float32) - times_seed(b, probe)
        car[k] = green.astype(jnp.bfloat16)
        for index, (chain, slab) in enumerate(far_on):
            if slab == slabs - 1:
                @pl.when(jnp.logical_and(low, i == index))
                def _(chain=chain):
                    send_car(chain - slabs).start()

        for index, (chain, slab) in enumerate(own_on):
            if slab == chain:
                @pl.when(i == far_count + index)
                def _(chain=chain):
                    if chain == slabs - 1:
                        @pl.when(linked)
                        def _():
                            for h in range(2):
                                send_block(h, seg + 1).start()

                    out[0, 0, chain] = car[chain, :, 0:width]
                    out[1, 0, chain] = car[chain, :, pad : pad + width]

        return carry

    lax.fori_loop(role * far_count, far_count + own_count, on_pass, 0)

    @pl.when(high)
    def _():
        for k in range(slabs):
            send_vec(k).wait_send()

    @pl.when(linked)
    def _():
        for h in range(2):
            send_block(h, seg + 1).wait_send()

    @pl.when(low)
    def _():
        for k in range(slabs):
            send_car(k).wait_send()

        def sent(j, carry):
            s, h = j // 2, j % 2

            @pl.when(goes_next(s, h))
            def _():
                ring_next(s, h).wait_send()

            @pl.when(goes_prev(s, h))
            def _():
                ring_prev(s, h).wait_send()

            return carry

        lax.fori_loop(0, ticks, sent, 0)


def local(nseg, n, energies, hamiltonian, coupling, seed_inverse, lead_green):
    slabs, order, _ = hamiltonian.shape
    width = lead_green.shape[3]
    pad = -(-width // LANES) * LANES
    wide = 2 * pad
    chains = 2 * slabs
    steps = n // 2
    vmem = pl.BlockSpec(memory_space=pltpu.VMEM)
    dma = pltpu.SemaphoreType.DMA
    bf16, f32 = jnp.bfloat16, jnp.float32
    return pl.pallas_call(
        functools.partial(kernel, nseg, n, width, pad),
        out_shape=jax.ShapeDtypeStruct((2, 1, slabs, order, width), bf16),
        in_specs=[pl.BlockSpec(memory_space=pltpu.SMEM)] + [vmem] * 4,
        out_specs=vmem,
        scratch_shapes=[
            pltpu.VMEM((slabs, order, order), bf16),
            pltpu.VMEM((n, 2, order // 2, wide), bf16),
            pltpu.VMEM((n, wide, chains * wide), bf16),
            pltpu.VMEM((chains, order, wide), bf16),
            pltpu.VMEM((chains, slabs, order, wide), bf16),
            pltpu.VMEM((chains, slabs, order, wide), f32),
            pltpu.VMEM((2, order // 2, chains * wide), f32),
            pltpu.VMEM((chains, order, wide), bf16),
            dma((slabs,)), dma((slabs,)), dma((slabs,)), dma((slabs,)),
            dma((2,)), dma((2,)),
            dma((steps, 2)), dma((steps, 2)), dma((steps, 2)), dma((steps, 2)),
        ],
        compiler_params=pltpu.CompilerParams(
            collective_id=0, has_side_effects=True, vmem_limit_bytes=60 * 2**20
        ),
    )(energies, hamiltonian, coupling, seed_inverse, lead_green)


def solution(mesh):
    in_specs = (
        P(),
        P("seg", None, None),
        P("seg", None, None),
        P(None, None, "seg", None, None),
        P(None, None, None, "tr"),
    )
    out_specs = P(None, None, "seg", None, "tr")
    body = functools.partial(local, mesh.shape["seg"], mesh.shape["tr"])
    return jax.shard_map(body, mesh=mesh, in_specs=in_specs, out_specs=out_specs, check_vma=False)
```

time: 629 us -> 79.6 us (0.13)
  waiting for transfers between devices: 435 us -> 0 us
  matrix products: 149 us -> 0 us
  Pallas kernels: 0 us -> 74.2 us
  between operations: 14.2 us -> 0.66 us
  local copies, waits for them, and re-layouts: 12.6 us -> 4.1 us
  other arithmetic: 7.53 us -> 0 us
    all_gather x8 -> x0, waiting for transfers between devices: 421 us -> none  [fold_columns(): piece = lax.all_gather(shard, 'tr', axis=2, tiled=True)]
    dot_general x72 -> x0, matrix products: 149 us -> none  [the longest x68 147 us: product(): return jnp.dot(left, right, preferred_element_type=jnp.float32)]
    pallas_call x0 -> x1, Pallas kernels: none -> 74.2 us  [local(): pl.pallas_call(functools.partial(kernel, nseg, n, width, pad), out_shape=...]
    ppermute x4 -> x0, waiting for transfers between devices: 13 us -> none  [passed_along(): lax.ppermute(value, axis, [(source, source + steps) for source in range(l...]
    unnamed x8 -> x1, local copies, waits for them, and re-layouts: 8.92 us -> 1.88 us
  transfers between devices with their start and end apart: 12 -> 0, of which waited for: 12 -> 0; matrix products, arithmetic and copies ran while one was open for 0% -> 0% of each run, Pallas kernels for 0% -> 0%
where the time goes in v1:
time: 79.6 us; the launch traced here: 78.9 us
  Pallas kernels  74.2 us (93%)
  local copies, waits for them, and re-layouts  4.1 us (5%)
    pallas_call x1, Pallas kernels, local(): pl.pallas_call(functools.partial(kernel, nseg, n, width, pad), out_shape=...  74.2 us
    pallas_call x1, local copies, waits for them, and re-layouts, local(): pl.pallas_call(functools.partial(kernel, nseg, n, width, pad), out_shape=...  2.21 us
    unnamed x1, local copies, waits for them, and re-layouts  1.88 us

profile of v1, /device:TPU:3, one launch (start us, length us, event | category | flops | bytes accessed | tf_op | source)
XLA Modules:
  0.0 78.9 jit_solution(2641062176592272195)
XLA Ops:
  0.7 1.9 %copy.6.lead = bf16[2,1,768,96]{3,2,1,0:T(8,128)(2,1)} copy(bf16[2,1,768,96]{2,3,1,0:T(8,128)(2,1)} %param.9) | data formatting | bytes 589824 | tf_op args[4]
  2.5 74.2 %shard_map.55 = bf16[2,1,2,768,96]{4,3,2,1,0:T(8,128)(2,1)} custom-call(f32[1]{0:T(128)S(6)} %copy.8.energies, bf16[2,768,768]{2,1,0:T(8,128)(2,1)} %ham.1, bf16[2,768,768]{2,1,0:T(8,128)(2,1)} %cpl.1, bf16[2,1,2,768,768]{4,3,2,1,0:T(8,128)(2,1)} %seed.1, bf16[2,1,768,96]{3,2,1,0:T(8,128)(2,1)} %copy.6.lead), custom_call_target="tpu_custom_call" | custom-call | tf_op jit(solution)/shard_map/pallas_call | solution.py:351
  76.7 2.2 %copy.7 = bf16[2,1,2,768,96]{3,4,2,1,0:T(8,128)(2,1)} copy(bf16[2,1,2,768,96]{4,3,2,1,0:T(8,128)(2,1)} %shard_map.55) | data formatting | bytes 1179648 | tf_op jit(solution)/shard_map/pallas_call | solution.py:351

commit v2 on v1

v2 whole, which is shorter than its diff:
```python
import functools

import jax
import jax.numpy as jnp
from jax import lax
from jax.experimental import pallas as pl
from jax.experimental.pallas import tpu as pltpu
from jax.sharding import PartitionSpec as P

broadening = 0.6
LANES = 128


def mm(left, right):
    return jnp.dot(left, right, preferred_element_type=jnp.float32)


def mm_left_turned(left, right):
    return lax.dot_general(
        left, right, (((0,), (0,)), ((), ())), preferred_element_type=jnp.float32
    )


def when(condition):
    if isinstance(condition, bool):
        return (lambda body: body()) if condition else (lambda body: None)
    return pl.when(condition)


def kernel(
    nseg, n, width, pad,
    energies, ham, cpl, seed, lead, out,
    hm, cp, sd, ct, gath, mix, vec, uvec, bias, acc, car, turned_out,
    in_sem, vs_sem, vr_sem, cs_sem, cr_sem, gs_sem, gr_sem, fs_sem, fr_sem, bs_sem, br_sem,
):
    slabs = ham.shape[0]
    order = ham.shape[1]
    half = order // 2
    steps = n // 2
    ticks = 2 * steps
    wide = 2 * pad
    chains = 2 * slabs
    top = chains - 1
    seg = lax.axis_index("seg")
    tr = lax.axis_index("tr")
    role = seg % 2
    low = role == 0
    high = role == 1
    first = seg == 0
    partner = seg + 1 - 2 * role
    linked = jnp.logical_and(high, seg + 1 < nseg)
    fed = jnp.logical_and(low, seg > 0)

    def inputs_of(b):
        pairs = (
            (seed.at[0, 0, b], sd.at[0, b]),
            (seed.at[1, 0, b], sd.at[1, b]),
            (cpl.at[b], cp.at[b]),
            (ham.at[b], hm.at[b]),
        )
        return [
            pltpu.make_async_copy(src, dst, in_sem.at[place, b])
            for place, (src, dst) in enumerate(pairs)
        ]

    for b in reversed(range(slabs)):
        for copy in inputs_of(b):
            copy.start()

    def place_of(t):
        odd = t % 2
        return odd * (n - 1 - t // 2) + (1 - odd) * (t // 2)

    def tr_at(position):
        position = (position + 2 * n) % n
        past = position // steps
        return (1 - past) * (2 * position) + past * (2 * (n - 1 - position) + 1)

    me = place_of(tr)
    following, preceding = tr_at(me + 1), tr_at(me - 1)

    barrier = pltpu.get_barrier_semaphore()

    def greet(s, t):
        pl.semaphore_signal(
            barrier, inc=1, device_id=(s, t), device_id_type=pl.DeviceIdType.MESH
        )

    greet(partner, tr)

    @pl.when(low)
    def _():
        greet(seg, following)
        greet(seg, preceding)

    @pl.when(fed)
    def _():
        greet(seg - 1, tr)

    @pl.when(linked)
    def _():
        greet(seg + 1, tr)

    peers = 1 + 2 * (1 - role) + jnp.where(jnp.logical_or(fed, linked), 1, 0)
    pl.semaphore_wait(barrier, peers)

    def remote(src, dst, send, recv, s, t):
        return pltpu.make_async_remote_copy(
            src_ref=src, dst_ref=dst, send_sem=send, recv_sem=recv,
            device_id=(s, t), device_id_type=pl.DeviceIdType.MESH,
        )

    def ring_next(s, h):
        owner = tr_at(me - s)
        return remote(
            gath.at[owner, h], gath.at[owner, h], fs_sem.at[s, h], fr_sem.at[s, h], seg, following
        )

    def ring_prev(s, h):
        owner = tr_at(me + s)
        return remote(
            gath.at[owner, h], gath.at[owner, h], bs_sem.at[s, h], br_sem.at[s, h], seg, preceding
        )

    def goes_next(s, h):
        return (s < steps - 1) | (h == 0)

    def goes_prev(s, h):
        return (s < steps - 1) | (h == 1)

    def ring_start(s, h):
        when(goes_next(s, h))(lambda: ring_next(s, h).start())
        when(goes_prev(s, h))(lambda: ring_prev(s, h).start())

    def tick(j):
        s, h = j // 2, j % 2
        when(goes_next(s, h))(lambda: ring_next(s, h).wait_recv())
        when(goes_prev(s, h))(lambda: ring_prev(s, h).wait_recv())
        when(s + 1 < steps)(lambda: ring_start(s + 1, h))

    def send_vec(k):
        return remote(
            vec.at[k], vec.at[slabs + k], vs_sem.at[k], vr_sem.at[k], partner, tr
        )

    def send_car(k):
        return remote(
            car.at[slabs + k], car.at[k], cs_sem.at[k], cr_sem.at[k], partner, tr
        )

    def send_block(h, s):
        return remote(turned_out.at[h], gath.at[tr, h], gs_sem.at[h], gr_sem.at[h], s, tr)

    @pl.when(first)
    def _():
        for h in range(2):
            for part in range(2):
                gath[tr, h, part * width : (part + 1) * width, :] = lead[
                    part, 0, :, h * half : (h + 1) * half
                ]
            ring_start(0, h)

    row = lax.broadcasted_iota(jnp.int32, (order, wide), 0)
    lane = lax.broadcasted_iota(jnp.int32, (order, wide), 1)
    chosen = jnp.logical_and(row == tr * width + lane, lane < width)
    unit = jnp.where(chosen, 1.0, 0.0).astype(jnp.bfloat16)
    for k in range(slabs):
        vec[k] = unit

    energy = energies[0]
    far = list(reversed(range(slabs, chains)))
    own = list(reversed(range(slabs)))

    def side_by_side(blocks):
        return blocks[0] if len(blocks) == 1 else jnp.concatenate(blocks, axis=1)

    def times_seed(b, value):
        by_real = mm(sd[0, b], value)
        by_imag = mm(sd[1, b], value)
        blocks = []
        for base in range(0, value.shape[1], wide):
            middle, end = base + pad, base + wide
            blocks.append(by_real[:, base:middle] - by_imag[:, middle:end])
            blocks.append(by_real[:, middle:end] + by_imag[:, base:middle])
        return side_by_side(blocks)

    def back_stage(ks, b, fresh=False, pause=lambda: None):
        if fresh:
            for copy in inputs_of(b):
                copy.wait()
            couple_turned = jnp.transpose(cp[b])
            ct[b] = couple_turned
        u = times_seed(b, side_by_side([vec[k] for k in ks])).astype(jnp.bfloat16)
        for place, k in enumerate(ks):
            uvec[k, b] = u[:, place * wide : (place + 1) * wide]
        pause()
        before = mm(ct[b], u).astype(jnp.bfloat16)
        onsite = mm(hm[b], u)
        for place, k in enumerate(ks):
            block = slice(place * wide, (place + 1) * wide)
            vec[k] = before[:, block]
            u32 = u[:, block].astype(jnp.float32)
            turned = jnp.concatenate([-u32[:, pad:], u32[:, :pad]], axis=1)
            bias[k, b] = energy * u32 + broadening * turned - onsite[:, block]
        pause()

    def back_loop(ks):
        def body(i, carry):
            back_stage(ks, slabs - 1 - i)
            return carry

        lax.fori_loop(0, slabs, body, 0)

    def on_stage(ks, b):
        value = side_by_side([car[k] for k in ks])
        bent = side_by_side([bias[k, b] for k in ks])
        probe = (bent - mm(cp[b], value)).astype(jnp.bfloat16)
        twice = 2.0 * side_by_side([uvec[k, b] for k in ks]).astype(jnp.float32)
        green = (twice - times_seed(b, probe)).astype(jnp.bfloat16)
        for place, k in enumerate(ks):
            car[k] = green[:, place * wide : (place + 1) * wide]

    def on_loop(ks, count):
        def body(b, carry):
            on_stage(ks, b)
            return carry

        lax.fori_loop(0, count, body, 0)

    def emit(k):
        block = car[k]
        parts = [
            jnp.transpose(block[:, base : base + pad])[:width] for base in (0, pad)
        ]
        if k == slabs - 1:
            @pl.when(linked)
            def _():
                for h in range(2):
                    for part in range(2):
                        turned_out[h, part * width : (part + 1) * width, :] = parts[part][
                            :, h * half : (h + 1) * half
                        ]
                    send_block(h, seg + 1).start()

        for part in range(2):
            out[part, 0, k] = parts[part]

    def build(ks):
        def body(t, carry):
            rows = pl.ds(pl.multiple_of(t * width, 16), width)
            for k in ks:
                block = vec[k, rows, :]
                base = k * wide
                mix[t, 0:width, base : base + wide] = block
                mix[t, width : 2 * width, base : base + pad] = -block[:, pad:]
                mix[t, width : 2 * width, base + pad : base + wide] = block[:, :pad]
            return carry

        lax.fori_loop(0, n, body, 0)

    def gathered_times(ks):
        start, stop = min(ks) * wide, (max(ks) + 1) * wide
        for h in range(2):
            total = mm_left_turned(gath[0, h], mix[0, :, start:stop])
            for t in range(1, n):
                total = total + mm_left_turned(gath[t, h], mix[t, :, start:stop])
            total = total.astype(jnp.bfloat16)
            for k in ks:
                car[k, h * half : (h + 1) * half, :] = total[
                    :, k * wide - start : (k + 1) * wide - start
                ]

    @pl.when(high)
    def _():
        for k in own:
            for b in reversed(range(k + 1)):
                back_stage([k], b, fresh=k == slabs - 1)
            send_vec(k).start()
        for k in own:
            send_car(k).wait_recv()
            on_loop([k], k + 1)
            emit(k)

    @pl.when(first)
    def _():
        waiting = list(range(ticks))

        def pause():
            if waiting:
                tick(waiting.pop(0))

        for b in own:
            back_stage(own[: slabs - b], b, fresh=True, pause=pause)
        send_vec(top - slabs).wait_recv()
        for b in own:
            back_stage([top], b, pause=pause)
        build([top])
        while waiting:
            pause()
        gathered_times([top])
        on_loop([top], slabs)
        send_car(top - slabs).start()
        for k in far[1:]:
            send_vec(k - slabs).wait_recv()
        back_loop(far[1:])
        build(far[1:] + own)
        gathered_times(far[1:] + own)
        on_loop(far[1:], slabs)
        for k in far[1:]:
            send_car(k - slabs).start()

    @pl.when(fed)
    def _():
        for b in own:
            back_stage(own[: slabs - b], b, fresh=True)
        for k in far:
            send_vec(k - slabs).wait_recv()
        back_loop(far)
        build(far + own)
        for h in range(2):
            send_block(h, seg).wait_recv()
            ring_start(0, h)
        for h in range(2):
            acc[h] = mm_left_turned(gath[tr, h], mix[tr])

        def add(owner, h):
            acc[h] = acc[h] + mm_left_turned(gath[owner, h], mix[owner])

        def arrive(j, carry):
            tick(j)
            s, h = j // 2, j % 2
            when(goes_next(s, h))(lambda: add(tr_at(me - 1 - s), h))
            when(goes_prev(s, h))(lambda: add(tr_at(me + 1 + s), h))
            return carry

        lax.fori_loop(0, ticks, arrive, 0)
        for k in range(chains):
            for h in range(2):
                car[k, h * half : (h + 1) * half, :] = acc[
                    h, :, k * wide : (k + 1) * wide
                ].astype(jnp.bfloat16)
        on_loop(far, slabs)
        for k in far:
            send_car(k - slabs).start()

    @pl.when(low)
    def _():
        for b in range(slabs):
            on_stage(own[: slabs - b], b)
            emit(b)

    @pl.when(high)
    def _():
        for k in range(slabs):
            send_vec(k).wait_send()

    @pl.when(linked)
    def _():
        for h in range(2):
            send_block(h, seg + 1).wait_send()

    @pl.when(low)
    def _():
        for k in range(slabs):
            send_car(k).wait_send()

        def sent(j, carry):
            s, h = j // 2, j % 2

            when(goes_next(s, h))(lambda: ring_next(s, h).wait_send())
            when(goes_prev(s, h))(lambda: ring_prev(s, h).wait_send())

            return carry

        lax.fori_loop(0, ticks, sent, 0)


def local(nseg, n, energies, hamiltonian, coupling, seed_inverse, lead_green):
    slabs, order, _ = hamiltonian.shape
    width = lead_green.shape[3]
    pad = -(-width // LANES) * LANES
    wide = 2 * pad
    chains = 2 * slabs
    steps = n // 2
    vmem = pl.BlockSpec(memory_space=pltpu.VMEM)
    anywhere = pl.BlockSpec(memory_space=pl.ANY)
    dma = pltpu.SemaphoreType.DMA
    bf16, f32 = jnp.bfloat16, jnp.float32
    turned = pl.pallas_call(
        functools.partial(kernel, nseg, n, width, pad),
        out_shape=jax.ShapeDtypeStruct((2, 1, slabs, width, order), bf16),
        in_specs=[pl.BlockSpec(memory_space=pltpu.SMEM)] + [anywhere] * 3 + [vmem],
        out_specs=vmem,
        scratch_shapes=[
            pltpu.VMEM((slabs, order, order), bf16),
            pltpu.VMEM((slabs, order, order), bf16),
            pltpu.VMEM((2, slabs, order, order), bf16),
            pltpu.VMEM((slabs, order, order), bf16),
            pltpu.VMEM((n, 2, 2 * width, order // 2), bf16),
            pltpu.VMEM((n, 2 * width, chains * wide), bf16),
            pltpu.VMEM((chains, order, wide), bf16),
            pltpu.VMEM((chains, slabs, order, wide), bf16),
            pltpu.VMEM((chains, slabs, order, wide), f32),
            pltpu.VMEM((2, order // 2, chains * wide), f32),
            pltpu.VMEM((chains, order, wide), bf16),
            pltpu.VMEM((2, 2 * width, order // 2), bf16),
            dma((4, slabs)),
            dma((slabs,)), dma((slabs,)), dma((slabs,)), dma((slabs,)),
            dma((2,)), dma((2,)),
            dma((steps, 2)), dma((steps, 2)), dma((steps, 2)), dma((steps, 2)),
        ],
        compiler_params=pltpu.CompilerParams(
            collective_id=0, has_side_effects=True, vmem_limit_bytes=60 * 2**20
        ),
    )(energies, hamiltonian, coupling, seed_inverse, jnp.swapaxes(lead_green, 2, 3))
    return jnp.swapaxes(turned, 3, 4)


def solution(mesh):
    in_specs = (
        P(),
        P("seg", None, None),
        P("seg", None, None),
        P(None, None, "seg", None, None),
        P(None, None, None, "tr"),
    )
    out_specs = P(None, None, "seg", None, "tr")
    body = functools.partial(local, mesh.shape["seg"], mesh.shape["tr"])
    return jax.shard_map(body, mesh=mesh, in_specs=in_specs, out_specs=out_specs, check_vma=False)
```

time: 79.6 us -> 64.8 us (0.81)
  Pallas kernels: 74.2 us -> 62 us
  local copies, waits for them, and re-layouts: 4.1 us -> 1.92 us
    pallas_call x1, Pallas kernels: 74.2 us -> 62 us  [local(): pl.pallas_call(functools.partial(kernel, nseg, n, width, pad), out_shape=...]
    pallas_call x1 -> x0, local copies, waits for them, and re-layouts: 2.21 us -> none  [local(): pl.pallas_call(functools.partial(kernel, nseg, n, width, pad), out_shape=...]
where the time goes in v2:
time: 64.8 us; the launch traced here: 64.6 us
  Pallas kernels  62 us (96%)
  local copies, waits for them, and re-layouts  1.92 us (3%)
  between operations  0.66 us (1%)
    pallas_call x1, Pallas kernels, local(): pl.pallas_call(functools.partial(kernel, nseg, n, width, pad), out_shape=...  62 us
    unnamed x1, local copies, waits for them, and re-layouts  1.92 us

profile of v2, /device:TPU:3, one launch (start us, length us, event | category | flops | bytes accessed | tf_op | source)
XLA Modules:
  0.0 64.6 jit_solution(16276775548404308824)
XLA Ops:
  0.7 62.0 %shard_map.55 = bf16[2,1,2,96,768]{4,3,2,1,0:T(8,128)(2,1)} custom-call(f32[1]{0:T(128)S(6)} %copy.7.energies, bf16[2,768,768]{2,1,0:T(8,128)(2,1)} %ham.1, bf16[2,768,768]{2,1,0:T(8,128)(2,1)} %cpl.1, bf16[2,1,2,768,768]{4,3,2,1,0:T(8,128)(2,1)} %seed.1, bf16[2,1,96,768]{3,2,1,0:T(8,128)(2,1)} %bitcast.3), custom_call_target="tpu_custom_call" | custom-call | tf_op jit(solution)/shard_map/pallas_call | solution.py:389
  62.7 1.9 %copy.8 = bf16[2,1,2,768,96]{3,4,2,1,0:T(8,128)(2,1)} copy(bf16[2,1,2,768,96]{3,4,2,1,0:T(8,128)(2,1)} %bitcast.2) | data formatting | bytes 1179648

commit v3 on v2

--- a/solution.py
+++ b/solution.py
@@ -30,7 +30,7 @@
 def kernel(
     nseg, n, width, pad,
     energies, ham, cpl, seed, lead, out,
-    hm, cp, sd, ct, gath, mix, vec, uvec, bias, acc, car, turned_out,
+    hm, cp, sd, ct, gath, mix, vec, uvec, bias, acc, car, turned_out, left, aff,
     in_sem, vs_sem, vr_sem, cs_sem, cr_sem, gs_sem, gr_sem, fs_sem, fr_sem, bs_sem, br_sem,
 ):
     slabs = ham.shape[0]
@@ -174,15 +174,18 @@
     def side_by_side(blocks):
         return blocks[0] if len(blocks) == 1 else jnp.concatenate(blocks, axis=1)
 
-    def times_seed(b, value):
-        by_real = mm(sd[0, b], value)
-        by_imag = mm(sd[1, b], value)
+    def times(real_part, imag_part, value, span):
+        by_real = mm(real_part, value)
+        by_imag = mm(imag_part, value)
         blocks = []
-        for base in range(0, value.shape[1], wide):
-            middle, end = base + pad, base + wide
+        for base in range(0, value.shape[1], span):
+            middle, end = base + span // 2, base + span
             blocks.append(by_real[:, base:middle] - by_imag[:, middle:end])
             blocks.append(by_real[:, middle:end] + by_imag[:, base:middle])
         return side_by_side(blocks)
+
+    def times_seed(b, value):
+        return times(sd[0, b], sd[1, b], value, wide)
 
     def back_stage(ks, b, fresh=False, pause=lambda: None):
         if fresh:
@@ -227,6 +230,49 @@
 
         lax.fori_loop(0, count, body, 0)
 
+    block_count = max(1, order // 256)
+    block_width = order // block_count
+
+    def left_start():
+        def body(i, carry):
+            cols = pl.ds(pl.multiple_of(i * block_width, 128), block_width)
+            couple = cp[0, :, cols]
+            for part in range(2):
+                left[part, 0, :, cols] = mm(sd[part, 0], couple).astype(jnp.bfloat16)
+            return carry
+
+        lax.fori_loop(0, block_count, body, 0)
+
+    def left_extend(b, i, pause=lambda place: None):
+        cols = pl.ds(pl.multiple_of(i * block_width, 128), block_width)
+        before = side_by_side([left[part, b - 1, :, cols] for part in range(2)])
+        coupled = mm(cp[b], before).astype(jnp.bfloat16)
+        pause(0)
+        after = times(sd[0, b], sd[1, b], coupled, 2 * block_width).astype(jnp.bfloat16)
+        left[0, b, :, cols] = after[:, :block_width]
+        left[1, b, :, cols] = after[:, block_width:]
+        pause(1)
+
+    def affine_stage(ks, b):
+        probe = side_by_side([bias[k, b] for k in ks])
+        if b > 0:
+            known = side_by_side([aff[k] for k in ks]).astype(jnp.bfloat16)
+            probe = probe - mm(cp[b], known)
+        twice = 2.0 * side_by_side([uvec[k, b] for k in ks]).astype(jnp.float32)
+        green = twice - times_seed(b, probe.astype(jnp.bfloat16))
+        for place, k in enumerate(ks):
+            aff[k] = green[:, place * wide : (place + 1) * wide]
+
+    def affine_loop(ks, b):
+        def body(i, carry):
+            affine_stage([ks[0] - i], b)
+            return carry
+
+        lax.fori_loop(0, len(ks), body, 0)
+
+    def settle(k, b):
+        car[k] = (aff[k] + times(left[0, b], left[1, b], car[k], wide)).astype(jnp.bfloat16)
+
     def emit(k):
         block = car[k]
         parts = [
@@ -276,9 +322,29 @@
             for b in reversed(range(k + 1)):
                 back_stage([k], b, fresh=k == slabs - 1)
             send_vec(k).start()
+
+    @pl.when(seg == 1)
+    def _():
         for k in own:
             send_car(k).wait_recv()
             on_loop([k], k + 1)
+            emit(k)
+
+    @pl.when(jnp.logical_and(high, seg > 1))
+    def _():
+        left_start()
+        affine_loop(own, 0)
+        for b in range(1, slabs):
+            affine_loop(own[: slabs - b], b)
+
+            def body(i, carry, b=b):
+                left_extend(b, i)
+                return carry
+
+            lax.fori_loop(0, block_count, body, 0)
+        for k in own:
+            send_car(k).wait_recv()
+            settle(k, k)
             emit(k)
 
     @pl.when(first)
@@ -308,6 +374,9 @@
         on_loop(far[1:], slabs)
         for k in far[1:]:
             send_car(k - slabs).start()
+        for b in range(slabs):
+            on_stage(own[: slabs - b], b)
+            emit(b)
 
     @pl.when(fed)
     def _():
@@ -317,6 +386,8 @@
             send_vec(k - slabs).wait_recv()
         back_loop(far)
         build(far + own)
+        left_start()
+        affine_loop(far + own, 0)
         for h in range(2):
             send_block(h, seg).wait_recv()
             ring_start(0, h)
@@ -326,28 +397,47 @@
         def add(owner, h):
             acc[h] = acc[h] + mm_left_turned(gath[owner, h], mix[owner])
 
-        def arrive(j, carry):
-            tick(j)
-            s, h = j // 2, j % 2
-            when(goes_next(s, h))(lambda: add(tr_at(me - 1 - s), h))
-            when(goes_prev(s, h))(lambda: add(tr_at(me + 1 + s), h))
-            return carry
-
-        lax.fori_loop(0, ticks, arrive, 0)
-        for k in range(chains):
+        def arrive(j):
+            @pl.when(j < ticks)
+            def _():
+                tick(j)
+                s, h = j // 2, j % 2
+                when(goes_next(s, h))(lambda: add(tr_at(me - 1 - s), h))
+                when(goes_prev(s, h))(lambda: add(tr_at(me + 1 + s), h))
+
+        done = 0
+        for b in range(1, slabs):
+            def affine_body(i, carry, b=b, done=done):
+                affine_stage([top - i], b)
+                arrive(done + i)
+                return carry
+
+            lax.fori_loop(0, chains - b, affine_body, 0)
+            done += chains - b
+
+            def left_body(i, carry, b=b, done=done):
+                left_extend(b, i, lambda place: arrive(done + 2 * i + place))
+                return carry
+
+            lax.fori_loop(0, block_count, left_body, 0)
+            done += 2 * block_count
+
+        def rest(j, carry):
+            arrive(j)
+            return carry
+
+        if done < ticks:
+            lax.fori_loop(done, ticks, rest, 0)
+        for k in far + own:
             for h in range(2):
                 car[k, h * half : (h + 1) * half, :] = acc[
                     h, :, k * wide : (k + 1) * wide
                 ].astype(jnp.bfloat16)
-        on_loop(far, slabs)
-        for k in far:
-            send_car(k - slabs).start()
-
-    @pl.when(low)
-    def _():
-        for b in range(slabs):
-            on_stage(own[: slabs - b], b)
-            emit(b)
+            settle(k, min(k, slabs - 1))
+            if k >= slabs:
+                send_car(k - slabs).start()
+            else:
+                emit(k)
 
     @pl.when(high)
     def _():
@@ -404,6 +494,8 @@
             pltpu.VMEM((2, order // 2, chains * wide), f32),
             pltpu.VMEM((chains, order, wide), bf16),
             pltpu.VMEM((2, 2 * width, order // 2), bf16),
+            pltpu.VMEM((2, slabs, order, order), bf16),
+            pltpu.VMEM((chains, order, wide), f32),
             dma((4, slabs)),
             dma((slabs,)), dma((slabs,)), dma((slabs,)), dma((slabs,)),
             dma((2,)), dma((2,)),

time: 64.8 us -> 61.4 us (0.948)
  Pallas kernels: 62 us -> 58.6 us
    pallas_call x1, Pallas kernels: 62 us -> 58.6 us  [local(): pl.pallas_call(functools.partial(kernel, nseg, n, width, pad), out_shape=...]
where the time goes in v3:
time: 61.4 us; the launch traced here: 61.2 us
  Pallas kernels  58.6 us (95%)
  local copies, waits for them, and re-layouts  1.92 us (3%)
  between operations  0.66 us (1%)
    pallas_call x1, Pallas kernels, local(): pl.pallas_call(functools.partial(kernel, nseg, n, width, pad), out_shape=...  58.6 us
    unnamed x1, local copies, waits for them, and re-layouts  1.92 us

profile of v3, /device:TPU:3, one launch (start us, length us, event | category | flops | bytes accessed | tf_op | source)
XLA Modules:
  0.0 61.2 jit_solution(6015035972386077859)
XLA Ops:
  0.7 58.6 %shard_map.55 = bf16[2,1,2,96,768]{4,3,2,1,0:T(8,128)(2,1)} custom-call(f32[1]{0:T(128)S(6)} %copy.7.energies, bf16[2,768,768]{2,1,0:T(8,128)(2,1)} %ham.1, bf16[2,768,768]{2,1,0:T(8,128)(2,1)} %cpl.1, bf16[2,1,2,768,768]{4,3,2,1,0:T(8,128)(2,1)} %seed.1, bf16[2,1,96,768]{3,2,1,0:T(8,128)(2,1)} %bitcast.3), custom_call_target="tpu_custom_call" | custom-call | tf_op jit(solution)/shard_map/pallas_call | solution.py:479
  59.2 1.9 %copy.8 = bf16[2,1,2,768,96]{3,4,2,1,0:T(8,128)(2,1)} copy(bf16[2,1,2,768,96]{3,4,2,1,0:T(8,128)(2,1)} %bitcast.2) | data formatting | bytes 1179648

commit v4 on v3

--- a/solution.py
+++ b/solution.py
@@ -233,25 +233,26 @@
     block_count = max(1, order // 256)
     block_width = order // block_count
 
+    def left_block(b, i):
+        cols = pl.ds(pl.multiple_of(i * block_width, 128), block_width)
+        couple = cp[b, :, cols]
+        for part in range(2):
+            left[part, b, :, cols] = mm(sd[part, b], couple).astype(jnp.bfloat16)
+
     def left_start():
         def body(i, carry):
-            cols = pl.ds(pl.multiple_of(i * block_width, 128), block_width)
-            couple = cp[0, :, cols]
-            for part in range(2):
-                left[part, 0, :, cols] = mm(sd[part, 0], couple).astype(jnp.bfloat16)
+            left_block(0, i)
             return carry
 
         lax.fori_loop(0, block_count, body, 0)
 
-    def left_extend(b, i, pause=lambda place: None):
+    def left_extend(b, i):
         cols = pl.ds(pl.multiple_of(i * block_width, 128), block_width)
         before = side_by_side([left[part, b - 1, :, cols] for part in range(2)])
         coupled = mm(cp[b], before).astype(jnp.bfloat16)
-        pause(0)
         after = times(sd[0, b], sd[1, b], coupled, 2 * block_width).astype(jnp.bfloat16)
         left[0, b, :, cols] = after[:, :block_width]
         left[1, b, :, cols] = after[:, block_width:]
-        pause(1)
 
     def affine_stage(ks, b):
         probe = side_by_side([bias[k, b] for k in ks])
@@ -269,6 +270,20 @@
             return carry
 
         lax.fori_loop(0, len(ks), body, 0)
+
+    def fold_stage(ks, b):
+        probe = side_by_side([bias[k, b] for k in ks]).astype(jnp.bfloat16)
+        twice = 2.0 * side_by_side([uvec[k, b] for k in ks]).astype(jnp.float32)
+        folded = twice - times_seed(b, probe)
+        for place, k in enumerate(ks):
+            bias[k, b] = folded[:, place * wide : (place + 1) * wide]
+
+    def fold_on(ks, b):
+        value = side_by_side([car[k] for k in ks])
+        folded = side_by_side([bias[k, b] for k in ks])
+        green = (folded + times(left[0, b], left[1, b], value, wide)).astype(jnp.bfloat16)
+        for place, k in enumerate(ks):
+            car[k] = green[:, place * wide : (place + 1) * wide]
 
     def settle(k, b):
         car[k] = (aff[k] + times(left[0, b], left[1, b], car[k], wide)).astype(jnp.bfloat16)
@@ -356,7 +371,7 @@
                 tick(waiting.pop(0))
 
         for b in own:
-            back_stage(own[: slabs - b], b, fresh=True, pause=pause)
+            back_stage(own[:1], b, fresh=True, pause=pause)
         send_vec(top - slabs).wait_recv()
         for b in own:
             back_stage([top], b, pause=pause)
@@ -368,7 +383,8 @@
         send_car(top - slabs).start()
         for k in far[1:]:
             send_vec(k - slabs).wait_recv()
-        back_loop(far[1:])
+        for b in own:
+            back_stage(far[1:] + [k for k in own[1:] if k >= b], b)
         build(far[1:] + own)
         gathered_times(far[1:] + own)
         on_loop(far[1:], slabs)
@@ -386,8 +402,12 @@
             send_vec(k - slabs).wait_recv()
         back_loop(far)
         build(far + own)
-        left_start()
-        affine_loop(far + own, 0)
+
+        def fold_pair(i, carry):
+            fold_stage([top - 2 * i, top - 2 * i - 1], 0)
+            return carry
+
+        lax.fori_loop(0, slabs, fold_pair, 0)
         for h in range(2):
             send_block(h, seg).wait_recv()
             ring_start(0, h)
@@ -405,22 +425,21 @@
                 when(goes_next(s, h))(lambda: add(tr_at(me - 1 - s), h))
                 when(goes_prev(s, h))(lambda: add(tr_at(me + 1 + s), h))
 
-        done = 0
+        def left_body(i, carry):
+            left_block(i // block_count, i % block_count)
+            arrive(i)
+            return carry
+
+        done = slabs * block_count
+        lax.fori_loop(0, done, left_body, 0)
         for b in range(1, slabs):
-            def affine_body(i, carry, b=b, done=done):
-                affine_stage([top - i], b)
+            def fold_body(i, carry, b=b, done=done):
+                fold_stage([top - i], b)
                 arrive(done + i)
                 return carry
 
-            lax.fori_loop(0, chains - b, affine_body, 0)
+            lax.fori_loop(0, chains - b, fold_body, 0)
             done += chains - b
-
-            def left_body(i, carry, b=b, done=done):
-                left_extend(b, i, lambda place: arrive(done + 2 * i + place))
-                return carry
-
-            lax.fori_loop(0, block_count, left_body, 0)
-            done += 2 * block_count
 
         def rest(j, carry):
             arrive(j)
@@ -433,11 +452,17 @@
                 car[k, h * half : (h + 1) * half, :] = acc[
                     h, :, k * wide : (k + 1) * wide
                 ].astype(jnp.bfloat16)
-            settle(k, min(k, slabs - 1))
-            if k >= slabs:
-                send_car(k - slabs).start()
-            else:
-                emit(k)
+
+        def fold_far(b, carry):
+            fold_on(far, b)
+            return carry
+
+        lax.fori_loop(0, slabs, fold_far, 0)
+        for k in far:
+            send_car(k - slabs).start()
+        for b in range(slabs):
+            fold_on(own[: slabs - b], b)
+            emit(b)
 
     @pl.when(high)
     def _():

time: 61.4 us -> 62.4 us (1.016)
  Pallas kernels: 58.6 us -> 59.6 us
    pallas_call x1, Pallas kernels: 58.6 us -> 59.6 us  [local(): pl.pallas_call(functools.partial(kernel, nseg, n, width, pad), out_shape=...]
where the time goes in v4:
time: 62.4 us; the launch traced here: 62.2 us
  Pallas kernels  59.6 us (96%)
  local copies, waits for them, and re-layouts  1.92 us (3%)
  between operations  0.66 us (1%)
    pallas_call x1, Pallas kernels, local(): pl.pallas_call(functools.partial(kernel, nseg, n, width, pad), out_shape=...  59.6 us
    unnamed x1, local copies, waits for them, and re-layouts  1.92 us

profile of v4, /device:TPU:3, one launch (start us, length us, event | category | flops | bytes accessed | tf_op | source)
XLA Modules:
  0.0 62.2 jit_solution(18240509391505550118)
XLA Ops:
  0.7 59.6 %shard_map.55 = bf16[2,1,2,96,768]{4,3,2,1,0:T(8,128)(2,1)} custom-call(f32[1]{0:T(128)S(6)} %copy.7.energies, bf16[2,768,768]{2,1,0:T(8,128)(2,1)} %ham.1, bf16[2,768,768]{2,1,0:T(8,128)(2,1)} %cpl.1, bf16[2,1,2,768,768]{4,3,2,1,0:T(8,128)(2,1)} %seed.1, bf16[2,1,96,768]{3,2,1,0:T(8,128)(2,1)} %bitcast.3), custom_call_target="tpu_custom_call" | custom-call | tf_op jit(solution)/shard_map/pallas_call | solution.py:504
  60.3 1.9 %copy.8 = bf16[2,1,2,768,96]{3,4,2,1,0:T(8,128)(2,1)} copy(bf16[2,1,2,768,96]{3,4,2,1,0:T(8,128)(2,1)} %bitcast.2) | data formatting | bytes 1179648

commit v5 on v4

--- a/solution.py
+++ b/solution.py
@@ -21,6 +21,13 @@
     )
 
 
+def pick(index, values):
+    total = jnp.int32(0)
+    for place, value in enumerate(values):
+        total = total + jnp.where(index == place, jnp.int32(value), jnp.int32(0))
+    return total
+
+
 def when(condition):
     if isinstance(condition, bool):
         return (lambda body: body()) if condition else (lambda body: None)
@@ -30,7 +37,7 @@
 def kernel(
     nseg, n, width, pad,
     energies, ham, cpl, seed, lead, out,
-    hm, cp, sd, ct, gath, mix, vec, uvec, bias, acc, car, turned_out, left, aff,
+    hm, cp, sd, ct, gath, mix, vec, uvec, bias, acc, car, turned_out, left, aff, held,
     in_sem, vs_sem, vr_sem, cs_sem, cr_sem, gs_sem, gr_sem, fs_sem, fr_sem, bs_sem, br_sem,
 ):
     slabs = ham.shape[0]
@@ -184,51 +191,48 @@
             blocks.append(by_real[:, middle:end] + by_imag[:, base:middle])
         return side_by_side(blocks)
 
-    def times_seed(b, value):
-        return times(sd[0, b], sd[1, b], value, wide)
-
-    def back_stage(ks, b, fresh=False, pause=lambda: None):
-        if fresh:
-            for copy in inputs_of(b):
-                copy.wait()
-            couple_turned = jnp.transpose(cp[b])
-            ct[b] = couple_turned
-        u = times_seed(b, side_by_side([vec[k] for k in ks])).astype(jnp.bfloat16)
-        for place, k in enumerate(ks):
-            uvec[k, b] = u[:, place * wide : (place + 1) * wide]
-        pause()
-        before = mm(ct[b], u).astype(jnp.bfloat16)
-        onsite = mm(hm[b], u)
-        for place, k in enumerate(ks):
-            block = slice(place * wide, (place + 1) * wide)
-            vec[k] = before[:, block]
-            u32 = u[:, block].astype(jnp.float32)
+    def by_halves(body):
+        def run(h, carry):
+            body(pl.ds(pl.multiple_of(h * half, 16), half))
+            return carry
+
+        lax.fori_loop(0, 2, run, 0)
+
+    def times_seed(b, rows, value):
+        return times(sd[0, b, rows, :], sd[1, b, rows, :], value, wide)
+
+    def twice(k, b, rows):
+        return 2.0 * uvec[k, b, rows, :].astype(jnp.float32)
+
+    def back_stage(k, b, pause=lambda place: None):
+        def seeded(rows):
+            uvec[k, b, rows, :] = times_seed(b, rows, vec[k]).astype(jnp.bfloat16)
+
+        by_halves(seeded)
+        pause(0)
+
+        def coupled(rows):
+            u = uvec[k, b]
+            vec[k, rows, :] = mm(ct[b, rows, :], u).astype(jnp.bfloat16)
+            u32 = uvec[k, b, rows, :].astype(jnp.float32)
             turned = jnp.concatenate([-u32[:, pad:], u32[:, :pad]], axis=1)
-            bias[k, b] = energy * u32 + broadening * turned - onsite[:, block]
-        pause()
-
-    def back_loop(ks):
-        def body(i, carry):
-            back_stage(ks, slabs - 1 - i)
-            return carry
-
-        lax.fori_loop(0, slabs, body, 0)
-
-    def on_stage(ks, b):
-        value = side_by_side([car[k] for k in ks])
-        bent = side_by_side([bias[k, b] for k in ks])
-        probe = (bent - mm(cp[b], value)).astype(jnp.bfloat16)
-        twice = 2.0 * side_by_side([uvec[k, b] for k in ks]).astype(jnp.float32)
-        green = (twice - times_seed(b, probe)).astype(jnp.bfloat16)
-        for place, k in enumerate(ks):
-            car[k] = green[:, place * wide : (place + 1) * wide]
-
-    def on_loop(ks, count):
-        def body(b, carry):
-            on_stage(ks, b)
-            return carry
-
-        lax.fori_loop(0, count, body, 0)
+            bias[k, b, rows, :] = energy * u32 + broadening * turned - mm(hm[b, rows, :], u)
+
+        by_halves(coupled)
+        pause(1)
+
+    def on_stage(k, b):
+        def probed(rows):
+            probe = bias[k, b, rows, :] - mm(cp[b, rows, :], car[k])
+            held[rows, :] = probe.astype(jnp.bfloat16)
+
+        by_halves(probed)
+
+        def finished(rows):
+            green = twice(k, b, rows) - times_seed(b, rows, held[...])
+            car[k, rows, :] = green.astype(jnp.bfloat16)
+
+        by_halves(finished)
 
     block_count = max(1, order // 256)
     block_width = order // block_count
@@ -250,43 +254,59 @@
         cols = pl.ds(pl.multiple_of(i * block_width, 128), block_width)
         before = side_by_side([left[part, b - 1, :, cols] for part in range(2)])
         coupled = mm(cp[b], before).astype(jnp.bfloat16)
-        after = times(sd[0, b], sd[1, b], coupled, 2 * block_width).astype(jnp.bfloat16)
-        left[0, b, :, cols] = after[:, :block_width]
-        left[1, b, :, cols] = after[:, block_width:]
-
-    def affine_stage(ks, b):
-        probe = side_by_side([bias[k, b] for k in ks])
-        if b > 0:
-            known = side_by_side([aff[k] for k in ks]).astype(jnp.bfloat16)
-            probe = probe - mm(cp[b], known)
-        twice = 2.0 * side_by_side([uvec[k, b] for k in ks]).astype(jnp.float32)
-        green = twice - times_seed(b, probe.astype(jnp.bfloat16))
-        for place, k in enumerate(ks):
-            aff[k] = green[:, place * wide : (place + 1) * wide]
+
+        def extended(rows):
+            after = times(sd[0, b, rows, :], sd[1, b, rows, :], coupled, 2 * block_width)
+            after = after.astype(jnp.bfloat16)
+            left[0, b, rows, cols] = after[:, :block_width]
+            left[1, b, rows, cols] = after[:, block_width:]
+
+        by_halves(extended)
+
+    def affine_stage(k, b):
+        if b == 0:
+            held[...] = bias[k, 0].astype(jnp.bfloat16)
+        else:
+            known = aff[k].astype(jnp.bfloat16)
+            held[...] = (bias[k, b] - mm(cp[b], known)).astype(jnp.bfloat16)
+
+        def finished(rows):
+            aff[k, rows, :] = twice(k, b, rows) - times_seed(b, rows, held[...])
+
+        by_halves(finished)
 
     def affine_loop(ks, b):
         def body(i, carry):
-            affine_stage([ks[0] - i], b)
+            affine_stage(ks[0] - i, b)
             return carry
 
         lax.fori_loop(0, len(ks), body, 0)
 
-    def fold_stage(ks, b):
-        probe = side_by_side([bias[k, b] for k in ks]).astype(jnp.bfloat16)
-        twice = 2.0 * side_by_side([uvec[k, b] for k in ks]).astype(jnp.float32)
-        folded = twice - times_seed(b, probe)
-        for place, k in enumerate(ks):
-            bias[k, b] = folded[:, place * wide : (place + 1) * wide]
-
-    def fold_on(ks, b):
-        value = side_by_side([car[k] for k in ks])
-        folded = side_by_side([bias[k, b] for k in ks])
-        green = (folded + times(left[0, b], left[1, b], value, wide)).astype(jnp.bfloat16)
-        for place, k in enumerate(ks):
-            car[k] = green[:, place * wide : (place + 1) * wide]
+    def fold_stage(k, b):
+        held[...] = bias[k, b].astype(jnp.bfloat16)
+
+        def folded(rows):
+            bias[k, b, rows, :] = twice(k, b, rows) - times_seed(b, rows, held[...])
+
+        by_halves(folded)
+
+    def fold_on(k, b):
+        held[...] = car[k]
+
+        def finished(rows):
+            value = times(left[0, b, rows, :], left[1, b, rows, :], held[...], wide)
+            car[k, rows, :] = (bias[k, b, rows, :] + value).astype(jnp.bfloat16)
+
+        by_halves(finished)
 
     def settle(k, b):
-        car[k] = (aff[k] + times(left[0, b], left[1, b], car[k], wide)).astype(jnp.bfloat16)
+        held[...] = car[k]
+
+        def finished(rows):
+            value = times(left[0, b, rows, :], left[1, b, rows, :], held[...], wide)
+            car[k, rows, :] = (aff[k, rows, :] + value).astype(jnp.bfloat16)
+
+        by_halves(finished)
 
     def emit(k):
         block = car[k]
@@ -321,29 +341,92 @@
 
     def gathered_times(ks):
         start, stop = min(ks) * wide, (max(ks) + 1) * wide
-        for h in range(2):
+
+        def body(h, carry):
             total = mm_left_turned(gath[0, h], mix[0, :, start:stop])
             for t in range(1, n):
                 total = total + mm_left_turned(gath[t, h], mix[t, :, start:stop])
             total = total.astype(jnp.bfloat16)
+            rows = pl.ds(pl.multiple_of(h * half, 16), half)
             for k in ks:
-                car[k, h * half : (h + 1) * half, :] = total[
-                    :, k * wide - start : (k + 1) * wide - start
-                ]
-
-    @pl.when(high)
-    def _():
-        for k in own:
-            for b in reversed(range(k + 1)):
-                back_stage([k], b, fresh=k == slabs - 1)
-            send_vec(k).start()
-
-    @pl.when(seg == 1)
-    def _():
-        for k in own:
-            send_car(k).wait_recv()
-            on_loop([k], k + 1)
-            emit(k)
+                car[k, rows, :] = total[:, k * wide - start : (k + 1) * wide - start]
+            return carry
+
+        lax.fori_loop(0, 2, body, 0)
+
+    def down(k):
+        return [(k, b) for b in reversed(range(min(k + 1, slabs)))]
+
+    main = down(slabs - 1) + down(top)
+    rest_own = [item for k in own[1:] for item in down(k)]
+    rest_far = [item for k in far[1:] for item in down(k)]
+    plan = main + rest_own + rest_far
+    last_tick = min(ticks, 2 * len(main))
+
+    def plan_pass(i):
+        k = pick(i, [item[0] for item in plan])
+        b = pick(i, [item[1] for item in plan])
+
+        @pl.when(i < slabs)
+        def _():
+            for copy in inputs_of(b):
+                copy.wait()
+            ct[b] = jnp.transpose(cp[b])
+
+        for index, (chain, slab) in enumerate(plan):
+            if chain >= slabs and slab == slabs - 1:
+                @pl.when(i == index)
+                def _(chain=chain):
+                    send_vec(chain - slabs).wait_recv()
+
+        def pause(place):
+            j = 2 * i + place
+
+            @pl.when(jnp.logical_and(first, j < last_tick))
+            def _():
+                tick(j)
+
+        back_stage(k, b, pause)
+        for index, (chain, slab) in enumerate(plan):
+            if chain < slabs and slab == 0:
+                @pl.when(jnp.logical_and(high, i == index))
+                def _(chain=chain):
+                    send_vec(chain).start()
+
+    def opening(i, carry):
+        plan_pass(jnp.where(jnp.logical_and(high, i >= slabs), i + slabs, i))
+        return carry
+
+    own_count = slabs + len(rest_own)
+    opening_count = jnp.where(high, own_count, jnp.where(first, len(main), len(plan)))
+    lax.fori_loop(0, opening_count, opening, 0)
+
+    onward = [(k, b) for k in far[1:] for b in range(slabs)]
+    far_rest = len(onward)
+    onward = onward + [(k, b) for k in own for b in range(k + 1)]
+
+    def onward_pass(i, carry):
+        k = pick(i, [item[0] for item in onward])
+        b = pick(i, [item[1] for item in onward])
+        for index, (chain, slab) in enumerate(onward):
+            if chain < slabs and slab == 0:
+                @pl.when(jnp.logical_and(high, i == index))
+                def _(chain=chain):
+                    send_car(chain).wait_recv()
+
+        on_stage(k, b)
+        for index, (chain, slab) in enumerate(onward):
+            if chain >= slabs and slab == slabs - 1:
+                @pl.when(i == index)
+                def _(chain=chain):
+                    send_car(chain - slabs).start()
+
+            if chain == slab:
+                @pl.when(i == index)
+                def _(chain=chain):
+                    emit(chain)
+
+        return carry
 
     @pl.when(jnp.logical_and(high, seg > 1))
     def _():
@@ -364,50 +447,44 @@
 
     @pl.when(first)
     def _():
-        waiting = list(range(ticks))
-
-        def pause():
-            if waiting:
-                tick(waiting.pop(0))
-
-        for b in own:
-            back_stage(own[:1], b, fresh=True, pause=pause)
-        send_vec(top - slabs).wait_recv()
-        for b in own:
-            back_stage([top], b, pause=pause)
         build([top])
-        while waiting:
-            pause()
+
+        def flush(j, carry):
+            tick(j)
+            return carry
+
+        if last_tick < ticks:
+            lax.fori_loop(last_tick, ticks, flush, 0)
         gathered_times([top])
-        on_loop([top], slabs)
+
+        def main_on(b, carry):
+            on_stage(top, b)
+            return carry
+
+        lax.fori_loop(0, slabs, main_on, 0)
         send_car(top - slabs).start()
-        for k in far[1:]:
-            send_vec(k - slabs).wait_recv()
-        for b in own:
-            back_stage(far[1:] + [k for k in own[1:] if k >= b], b)
+
+        def later(i, carry):
+            plan_pass(i)
+            return carry
+
+        lax.fori_loop(len(main), len(plan), later, 0)
         build(far[1:] + own)
         gathered_times(far[1:] + own)
-        on_loop(far[1:], slabs)
-        for k in far[1:]:
-            send_car(k - slabs).start()
-        for b in range(slabs):
-            on_stage(own[: slabs - b], b)
-            emit(b)
+
+    @pl.when(seg < 2)
+    def _():
+        lax.fori_loop(role * far_rest, len(onward), onward_pass, 0)
 
     @pl.when(fed)
     def _():
-        for b in own:
-            back_stage(own[: slabs - b], b, fresh=True)
-        for k in far:
-            send_vec(k - slabs).wait_recv()
-        back_loop(far)
         build(far + own)
 
-        def fold_pair(i, carry):
-            fold_stage([top - 2 * i, top - 2 * i - 1], 0)
-            return carry
-
-        lax.fori_loop(0, slabs, fold_pair, 0)
+        def fold_one(i, carry):
+            fold_stage(top - i, 0)
+            return carry
+
+        lax.fori_loop(0, chains, fold_one, 0)
         for h in range(2):
             send_block(h, seg).wait_recv()
             ring_start(0, h)
@@ -434,7 +511,7 @@
         lax.fori_loop(0, done, left_body, 0)
         for b in range(1, slabs):
             def fold_body(i, carry, b=b, done=done):
-                fold_stage([top - i], b)
+                fold_stage(top - i, b)
                 arrive(done + i)
                 return carry
 
@@ -453,16 +530,27 @@
                     h, :, k * wide : (k + 1) * wide
                 ].astype(jnp.bfloat16)
 
-        def fold_far(b, carry):
-            fold_on(far, b)
-            return carry
-
-        lax.fori_loop(0, slabs, fold_far, 0)
-        for k in far:
-            send_car(k - slabs).start()
-        for b in range(slabs):
-            fold_on(own[: slabs - b], b)
-            emit(b)
+        closing = [(k, b) for k in far for b in range(slabs)]
+        closing = closing + [(k, b) for k in own for b in range(k + 1)]
+
+        def closing_pass(i, carry):
+            k = pick(i, [item[0] for item in closing])
+            b = pick(i, [item[1] for item in closing])
+            fold_on(k, b)
+            for index, (chain, slab) in enumerate(closing):
+                if chain >= slabs and slab == slabs - 1:
+                    @pl.when(i == index)
+                    def _(chain=chain):
+                        send_car(chain - slabs).start()
+
+                if chain == slab:
+                    @pl.when(i == index)
+                    def _(chain=chain):
+                        emit(chain)
+
+            return carry
+
+        lax.fori_loop(0, len(closing), closing_pass, 0)
 
     @pl.when(high)
     def _():
@@ -521,6 +609,7 @@
             pltpu.VMEM((2, 2 * width, order // 2), bf16),
             pltpu.VMEM((2, slabs, order, order), bf16),
             pltpu.VMEM((chains, order, wide), f32),
+            pltpu.VMEM((order, wide), bf16),
             dma((4, slabs)),
             dma((slabs,)), dma((slabs,)), dma((slabs,)), dma((slabs,)),
             dma((2,)), dma((2,)),

time: 62.4 us -> 65.7 us (1.053)
  Pallas kernels: 59.6 us -> 62.7 us
    pallas_call x1, Pallas kernels: 59.6 us -> 62.7 us  [local(): pl.pallas_call(functools.partial(kernel, nseg, n, width, pad), out_shape=...]
where the time goes in v5:
time: 65.7 us; the launch traced here: 65.3 us
  Pallas kernels  62.7 us (95%)
  local copies, waits for them, and re-layouts  1.92 us (3%)
  between operations  0.66 us (1%)
    pallas_call x1, Pallas kernels, local(): pl.pallas_call(functools.partial(kernel, nseg, n, width, pad), out_shape=...  62.7 us
    unnamed x1, local copies, waits for them, and re-layouts  1.92 us

profile of v5, /device:TPU:3, one launch (start us, length us, event | category | flops | bytes accessed | tf_op | source)
XLA Modules:
  0.0 65.3 jit_solution(4298606848428692310)
XLA Ops:
  0.7 62.7 %shard_map.55 = bf16[2,1,2,96,768]{4,3,2,1,0:T(8,128)(2,1)} custom-call(f32[1]{0:T(128)S(6)} %copy.7.energies, bf16[2,768,768]{2,1,0:T(8,128)(2,1)} %ham.1, bf16[2,768,768]{2,1,0:T(8,128)(2,1)} %cpl.1, bf16[2,1,2,768,768]{4,3,2,1,0:T(8,128)(2,1)} %seed.1, bf16[2,1,96,768]{3,2,1,0:T(8,128)(2,1)} %bitcast.3), custom_call_target="tpu_custom_call" | custom-call | tf_op jit(solution)/shard_map/pallas_call | solution.py:592
  63.3 1.9 %copy.8 = bf16[2,1,2,768,96]{3,4,2,1,0:T(8,128)(2,1)} copy(bf16[2,1,2,768,96]{3,4,2,1,0:T(8,128)(2,1)} %bitcast.2) | data formatting | bytes 1179648
